TPU v7x, 128 devices: a whole 4x4x4 slice. The times are simulated.
128 devices in a mesh: dp: 8 (over x, core), shard: 16 (over y, z).
Axes of the slice: x: 4, y: 4, z: 4, core: 2. Of those that a mesh axis runs over, the one named last changes fastest.
Arguments:
- source: bfloat16 [128, 384, 512], P(('dp', 'shard')), may hold values from -6 to 6
- target: bfloat16 [128, 384, 512], P(('dp', 'shard')), may hold values from -6 to 6
- source_lengths: int32 [128, 5], P(('dp', 'shard')), may hold values from 1 to 192, 384 in all within a row
- target_lengths: int32 [128, 5], P(('dp', 'shard')), may hold values from 1 to 192, 384 in all within a row
- lang_ids: int32 [128, 5], P(('dp', 'shard')), may hold values from 0 to 99
- out_cotangent: bfloat16 [128, 384, 512], P(('dp', 'shard')), may hold values from -6 to 6
- enc_attn: bfloat16 [4, 512, 512], P(None, ('dp', 'shard')), as said below
- enc_vectors: bfloat16 [8, 512], P(None, ('dp', 'shard'))
- enc_w_in: bfloat16 [512, 2048], P(('dp', 'shard')), may hold values from -0.25 to 0.25
- enc_b_in: bfloat16 [2048], P(('dp', 'shard')), may hold values from -4 to 4
- enc_w_out: bfloat16 [2048, 512], P(('dp', 'shard')), may hold values from -0.125 to 0.125
- dec_self: bfloat16 [4, 512, 512], P(None, ('dp', 'shard')), as said below
- dec_cross: bfloat16 [4, 512, 512], P(None, ('dp', 'shard')), as said below
- dec_vectors: bfloat16 [13, 512], P(None, ('dp', 'shard'))
- dec_w_in: bfloat16 [512, 2048], P(('dp', 'shard')), may hold values from -0.25 to 0.25
- dec_b_in: bfloat16 [2048], P(('dp', 'shard')), may hold values from -4 to 4
- dec_w_out: bfloat16 [2048, 512], P(('dp', 'shard')), may hold values from -0.125 to 0.125
- lang_table: bfloat16 [100, 512], P(None, ('dp', 'shard')), may hold values from -6 to 6
Outputs:
- dec_out: bfloat16 [128, 384, 512], P(('dp', 'shard'))
- grad_source: float32 [128, 384, 512], P(('dp', 'shard'))
- grad_target: float32 [128, 384, 512], P(('dp', 'shard'))
- grad_enc_attn: float32 [4, 512, 512], P(None, ('dp', 'shard'))
- grad_enc_vectors: float32 [8, 512], P(None, ('dp', 'shard'))
- grad_enc_w_in: float32 [512, 2048], P(('dp', 'shard'))
- grad_enc_b_in: float32 [2048], P(('dp', 'shard'))
- grad_enc_w_out: float32 [2048, 512], P(('dp', 'shard'))
- grad_dec_self: float32 [4, 512, 512], P(None, ('dp', 'shard'))
- grad_dec_cross: float32 [4, 512, 512], P(None, ('dp', 'shard'))
- grad_dec_vectors: float32 [13, 512], P(None, ('dp', 'shard'))
- grad_dec_w_in: float32 [512, 2048], P(('dp', 'shard'))
- grad_dec_b_in: float32 [2048], P(('dp', 'shard'))
- grad_dec_w_out: float32 [2048, 512], P(('dp', 'shard'))
- grad_lang_table: float32 [100, 512], P(None, ('dp', 'shard'))
Inputs may be any that keep to these rules, and one draw needn't show every extreme that they name: `source_lengths`: each row's entries sum to 384; the first 4 are document lengths, the last is the row's padding; some entry equals 192. `target_lengths`: as for source_lengths, drawn independently. `enc_attn`: projection matrices stacked as query, key, value, output. `dec_self`: projection matrices stacked as query, key, value, output. `dec_cross`: projection matrices stacked as query, key, value, output.
All inputs are finite; a program needn't handle non-finite values.
Results may differ from a plain program's by a relative error of at most 0.022.
Values may be sent and summed in bfloat16 or wider, within the bound.
No kernel may reach another device: no remote copies, remote signals or barrier semaphores. Data moves between devices by JAX's collectives and lax.ppermute only.
A program may use at most 192 MiB of HBM per device.

v0:
```python
import math

import jax
import jax.numpy as jnp
from jax import lax
from jax.sharding import PartitionSpec as P

D = 512
HEADS = 8
HEAD_DIM = 64
LANGS = 100
SEQ = 384
DOCS = 5


EPSILON = 1e-05
NEGATIVE = -1000000000.0
HIGHEST = lax.Precision.HIGHEST


def project(left, right):
    return jnp.dot(left, right, preferred_element_type=jnp.float32)


def outer_sum(left, right):
    return lax.dot_general(
        left, right, (((0,), (0,)), ((), ())), preferred_element_type=jnp.float32
    )


def back_project(grad, weight):
    return lax.dot_general(
        grad, weight, (((1,), (1,)), ((), ())), preferred_element_type=jnp.float32
    )


def column_sum(grad):
    return jnp.sum(grad.astype(jnp.float32), axis=0)


def layer_norm(values, gain, shift):
    center = values - jnp.mean(values, axis=-1, keepdims=True)
    spread = jnp.mean(center * center, axis=-1, keepdims=True)
    return center * lax.rsqrt(spread + EPSILON) * gain + shift


def norm_back(values, gain, shift, grad):
    _, pull = jax.vjp(layer_norm, values, gain.astype(jnp.float32), shift.astype(jnp.float32))
    return pull(grad)


def doc_index(lengths):
    ends = jnp.cumsum(lengths)
    positions = jnp.arange(SEQ, dtype=jnp.int32)
    return jnp.sum((positions[:, None] >= ends[None, :]).astype(jnp.int32), axis=1)


def heads(flat):
    return flat.reshape(flat.shape[0], HEADS, HEAD_DIM)


def masked_scores(query, keys, mask):
    scores = jnp.einsum(
        "qhd,khd->hqk", heads(query), heads(keys), preferred_element_type=jnp.float32
    )
    return jnp.where(mask[None], scores, NEGATIVE)


def attend_fwd(query_in, memory, weights, bias_q, bias_v, bias_o, mask):
    scale = HEAD_DIM ** (-0.5)
    query = (scale * (project(query_in, weights[0]) + bias_q)).astype(jnp.bfloat16)
    keys = project(memory, weights[1]).astype(jnp.bfloat16)
    values = (project(memory, weights[2]) + bias_v).astype(jnp.bfloat16)
    scores = masked_scores(query, keys, mask)
    row_max = jnp.max(scores, axis=-1, keepdims=True)
    expd = jnp.exp(scores - row_max)
    total = jnp.sum(expd, axis=-1, keepdims=True)
    attn_probs = (expd / total).astype(jnp.bfloat16)
    context = jnp.einsum(
        "hqk,khd->qhd", attn_probs, heads(values), preferred_element_type=jnp.float32
    )
    context = context.reshape(query.shape[0], D).astype(jnp.bfloat16)
    branch = project(context, weights[3]) + bias_o
    return (branch, (query, keys, values, row_max + jnp.log(total), context))


def attend_bwd(grad, query_in, memory, weights, kept, mask):
    query, keys, values, log_total, context = kept
    scale = HEAD_DIM ** (-0.5)
    rows = query.shape[0]
    grad_out = grad.astype(jnp.bfloat16)
    grad_wo = outer_sum(context, grad_out)
    grad_bo = column_sum(grad_out)
    grad_ctx = back_project(grad_out, weights[3]).astype(jnp.bfloat16)
    attn_probs = jnp.exp(masked_scores(query, keys, mask) - log_total)
    probs_low = attn_probs.astype(jnp.bfloat16)
    grad_probs = jnp.einsum(
        "qhd,khd->hqk", heads(grad_ctx), heads(values), preferred_element_type=jnp.float32
    )
    grad_scores = attn_probs * (
        grad_probs - jnp.sum(attn_probs * grad_probs, axis=-1, keepdims=True)
    )
    grad_scores = grad_scores.astype(jnp.bfloat16)
    grad_query = jnp.einsum(
        "hqk,khd->qhd", grad_scores, heads(keys), preferred_element_type=jnp.float32
    )
    grad_query = grad_query.reshape(rows, D).astype(jnp.bfloat16)
    grad_keys = jnp.einsum(
        "hqk,qhd->khd", grad_scores, heads(query), preferred_element_type=jnp.float32
    )
    grad_keys = grad_keys.reshape(keys.shape[0], D).astype(jnp.bfloat16)
    grad_values = jnp.einsum(
        "hqk,qhd->khd", probs_low, heads(grad_ctx), preferred_element_type=jnp.float32
    )
    grad_values = grad_values.reshape(keys.shape[0], D).astype(jnp.bfloat16)
    grad_wq = scale * outer_sum(query_in, grad_query)
    grad_bq = scale * column_sum(grad_query)
    grad_wk = outer_sum(memory, grad_keys)
    grad_wv = outer_sum(memory, grad_values)
    grad_bv = column_sum(grad_values)
    grad_in = scale * back_project(grad_query, weights[0])
    grad_mem = back_project(grad_keys, weights[1]) + back_project(grad_values, weights[2])
    matrices = jnp.stack([grad_wq, grad_wk, grad_wv, grad_wo])
    return (grad_in, grad_mem, matrices, grad_bq, grad_bv, grad_bo)


def feed_fwd(inputs, w_in, b_in, w_out, b_out):
    hidden = project(inputs, w_in) + b_in
    active = jax.nn.silu(hidden).astype(jnp.bfloat16)
    return (project(active, w_out) + b_out, (hidden, active))


def feed_bwd(grad, inputs, w_in, w_out, kept):
    hidden, active = kept
    grad_out = grad.astype(jnp.bfloat16)
    grad_w_out = outer_sum(active, grad_out)
    grad_b_out = column_sum(grad_out)
    grad_active = back_project(grad_out, w_out)
    _, pull = jax.vjp(jax.nn.silu, hidden)
    grad_hidden = pull(grad_active)[0].astype(jnp.bfloat16)
    grad_w_in = outer_sum(inputs, grad_hidden)
    grad_b_in = column_sum(grad_hidden)
    return (back_project(grad_hidden, w_in), grad_w_in, grad_b_in, grad_w_out, grad_b_out)


def encoder_fwd(source_row, weights, mask):
    attn, vectors, w_in, b_in, w_out = weights
    normed = layer_norm(source_row, vectors[0], vectors[1]).astype(jnp.bfloat16)
    branch, attn_kept = attend_fwd(normed, normed, attn, vectors[2], vectors[3], vectors[4], mask)
    middle = source_row + branch
    normed_two = layer_norm(middle, vectors[5], vectors[6]).astype(jnp.bfloat16)
    branch_two, feed_kept = feed_fwd(normed_two, w_in, b_in, w_out, vectors[7])
    return (middle + branch_two, (normed, attn_kept, middle, normed_two, feed_kept))


def encoder_bwd(grad, source_row, weights, kept, mask):
    attn, vectors, w_in, b_in, w_out = weights
    normed, attn_kept, middle, normed_two, feed_kept = kept
    grad_normed_two, grad_w_in, grad_b_in, grad_w_out, grad_b_two = feed_bwd(
        grad, normed_two, w_in, w_out, feed_kept
    )
    grad_mid_norm, gain_two, shift_two = norm_back(middle, vectors[5], vectors[6], grad_normed_two)
    grad_middle = grad + grad_mid_norm
    grad_in, grad_mem, matrices, grad_bq, grad_bv, grad_bo = attend_bwd(
        grad_middle, normed, normed, attn, attn_kept, mask
    )
    grad_src_norm, gain_one, shift_one = norm_back(
        source_row, vectors[0], vectors[1], grad_in + grad_mem
    )
    grad_vectors = jnp.stack(
        [gain_one, shift_one, grad_bq, grad_bv, grad_bo, gain_two, shift_two, grad_b_two]
    )
    return (grad_middle + grad_src_norm, (matrices, grad_vectors, grad_w_in, grad_b_in, grad_w_out))


def decoder_fwd(target_row, memory, weights, lang_onehot, self_mask, cross_mask):
    self_w, cross_w, vectors, w_in, b_in, w_out, table = weights
    start = target_row + project(lang_onehot, table)
    normed = layer_norm(start, vectors[0], vectors[1]).astype(jnp.bfloat16)
    branch, self_kept = attend_fwd(
        normed, normed, self_w, vectors[2], vectors[3], vectors[4], self_mask
    )
    first = start + branch
    normed_two = layer_norm(first, vectors[5], vectors[6]).astype(jnp.bfloat16)
    branch_two, cross_kept = attend_fwd(
        normed_two, memory, cross_w, vectors[7], vectors[8], vectors[9], cross_mask
    )
    second = first + branch_two
    normed_three = layer_norm(second, vectors[10], vectors[11]).astype(jnp.bfloat16)
    branch_three, feed_kept = feed_fwd(normed_three, w_in, b_in, w_out, vectors[12])
    kept = (
        start,
        normed,
        self_kept,
        first,
        normed_two,
        cross_kept,
        second,
        normed_three,
        feed_kept,
    )
    return (second + branch_three, kept)


def decoder_bwd(grad, memory, weights, kept, lang_onehot, self_mask, cross_mask):
    self_w, cross_w, vectors, w_in, b_in, w_out, table = weights
    start, normed, self_kept, first, normed_two, cross_kept, second, normed_three, feed_kept = kept
    grad_normed_three, grad_w_in, grad_b_in, grad_w_out, grad_b_three = feed_bwd(
        grad, normed_three, w_in, w_out, feed_kept
    )
    grad_sec_norm, gain_three, shift_three = norm_back(
        second, vectors[10], vectors[11], grad_normed_three
    )
    grad_second = grad + grad_sec_norm
    cross_in, cross_mem, cross_mats, cross_bq, cross_bv, cross_bo = attend_bwd(
        grad_second, normed_two, memory, cross_w, cross_kept, cross_mask
    )
    grad_first_norm, gain_two, shift_two = norm_back(first, vectors[5], vectors[6], cross_in)
    grad_first = grad_second + grad_first_norm
    self_in, self_mem, self_mats, self_bq, self_bv, self_bo = attend_bwd(
        grad_first, normed, normed, self_w, self_kept, self_mask
    )
    grad_start_norm, gain_one, shift_one = norm_back(
        start, vectors[0], vectors[1], self_in + self_mem
    )
    grad_start = grad_first + grad_start_norm
    grad_table = lax.dot_general(
        lang_onehot.astype(jnp.float32),
        grad_start,
        (((0,), (0,)), ((), ())),
        precision=HIGHEST,
        preferred_element_type=jnp.float32,
    )
    grad_vectors = jnp.stack(
        [
            gain_one,
            shift_one,
            self_bq,
            self_bv,
            self_bo,
            gain_two,
            shift_two,
            cross_bq,
            cross_bv,
            cross_bo,
            gain_three,
            shift_three,
            grad_b_three,
        ]
    )
    grads = (self_mats, cross_mats, grad_vectors, grad_w_in, grad_b_in, grad_w_out, grad_table)
    return (grad_start, cross_mem, grads)


def pack_rows(grads, dims, count):
    pieces = []
    for grad, axis_dim in zip(grads, dims):
        moved = jnp.moveaxis(grad, axis_dim, 0)
        pieces.append(moved.reshape(count, -1))
    return jnp.concatenate(pieces, axis=1)


def unpack_row(flat, grads, dims, count):
    results = []
    offset = 0
    for grad, axis_dim in zip(grads, dims):
        others = tuple((extent for index, extent in enumerate(grad.shape) if index != axis_dim))
        moved_shape = (grad.shape[axis_dim] // count,) + others
        amount = math.prod(moved_shape)
        piece = flat[0, offset : offset + amount].reshape(moved_shape)
        offset = offset + amount
        results.append(jnp.moveaxis(piece, 0, axis_dim))
    return tuple(results)


def pack_local(shards, dims):
    pieces = []
    for shard_piece, axis_dim in zip(shards, dims):
        moved = jnp.moveaxis(shard_piece, axis_dim, 0)
        pieces.append(moved.reshape(1, -1))
    return jnp.concatenate(pieces, axis=1)


def unpack_full(gathered, shards, dims, count):
    results = []
    offset = 0
    for shard_piece, axis_dim in zip(shards, dims):
        others = tuple(
            (extent for index, extent in enumerate(shard_piece.shape) if index != axis_dim)
        )
        moved_shape = (shard_piece.shape[axis_dim],) + others
        amount = math.prod(moved_shape)
        piece = gathered[:, offset : offset + amount].reshape(
            (count * shard_piece.shape[axis_dim],) + others
        )
        offset = offset + amount
        results.append(jnp.moveaxis(piece, 0, axis_dim))
    return tuple(results)


def collect(shards, dims):
    count = lax.axis_size("dp") * lax.axis_size("shard")
    packed = pack_local(shards, dims)
    gathered = lax.all_gather(packed, ("dp", "shard"), axis=0, tiled=True)
    return unpack_full(gathered, shards, dims, count)


def spread(grads, dims):
    count = lax.axis_size("dp") * lax.axis_size("shard")
    owned = lax.psum_scatter(
        pack_rows(grads, dims, count), ("dp", "shard"), scatter_dimension=0, tiled=True
    )
    return unpack_row(owned, grads, dims, count)


def per_device(
    source,
    target,
    source_lengths,
    target_lengths,
    lang_ids,
    out_cotangent,
    enc_attn,
    enc_vectors,
    enc_w_in,
    enc_b_in,
    enc_w_out,
    dec_self,
    dec_cross,
    dec_vectors,
    dec_w_in,
    dec_b_in,
    dec_w_out,
    lang_table,
):
    enc_dims = (1, 1, 0, 0, 0)
    dec_dims = (1, 1, 1, 0, 0, 0, 1)
    enc_shards = (enc_attn, enc_vectors, enc_w_in, enc_b_in, enc_w_out)
    dec_shards = (dec_self, dec_cross, dec_vectors, dec_w_in, dec_b_in, dec_w_out, lang_table)
    source_row = source[0].astype(jnp.float32)
    target_row = target[0].astype(jnp.float32)
    source_doc = doc_index(source_lengths[0])
    target_doc = doc_index(target_lengths[0])
    positions = jnp.arange(SEQ, dtype=jnp.int32)
    enc_mask = source_doc[:, None] == source_doc[None, :]
    self_mask = (target_doc[:, None] == target_doc[None, :]) & (
        positions[None, :] <= positions[:, None]
    )
    cross_mask = target_doc[:, None] == source_doc[None, :]
    doc_onehot = target_doc[:, None] == jnp.arange(DOCS, dtype=jnp.int32)[None, :]
    lang_rows = jnp.sum(jnp.where(doc_onehot, lang_ids[0][None, :], 0), axis=1)
    lang_onehot = (lang_rows[:, None] == jnp.arange(LANGS, dtype=jnp.int32)[None, :]).astype(
        jnp.bfloat16
    )
    enc_full = collect(enc_shards, enc_dims)
    encoded, enc_kept = encoder_fwd(source_row, enc_full, enc_mask)
    memory = encoded.astype(jnp.bfloat16)
    dec_full = collect(dec_shards, dec_dims)
    final, dec_kept = decoder_fwd(target_row, memory, dec_full, lang_onehot, self_mask, cross_mask)
    dec_again = collect(dec_shards, dec_dims)
    grad_start, grad_memory, dec_grads = decoder_bwd(
        out_cotangent[0].astype(jnp.float32),
        memory,
        dec_again,
        dec_kept,
        lang_onehot,
        self_mask,
        cross_mask,
    )
    dec_parts = spread(dec_grads, dec_dims)
    enc_again = collect(enc_shards, enc_dims)
    grad_src_row, enc_grads = encoder_bwd(grad_memory, source_row, enc_again, enc_kept, enc_mask)
    enc_parts = spread(enc_grads, enc_dims)
    return (
        final.astype(jnp.bfloat16)[None],
        grad_src_row[None],
        grad_start[None],
        enc_parts[0],
        enc_parts[1],
        enc_parts[2],
        enc_parts[3],
        enc_parts[4],
        dec_parts[0],
        dec_parts[1],
        dec_parts[2],
        dec_parts[3],
        dec_parts[4],
        dec_parts[5],
        dec_parts[6],
    )


def solution(mesh):
    in_specs = (
        P(("dp", "shard"), None, None),
        P(("dp", "shard"), None, None),
        P(("dp", "shard"), None),
        P(("dp", "shard"), None),
        P(("dp", "shard"), None),
        P(("dp", "shard"), None, None),
        P(None, ("dp", "shard"), None),
        P(None, ("dp", "shard")),
        P(("dp", "shard"), None),
        P(("dp", "shard")),
        P(("dp", "shard"), None),
        P(None, ("dp", "shard"), None),
        P(None, ("dp", "shard"), None),
        P(None, ("dp", "shard")),
        P(("dp", "shard"), None),
        P(("dp", "shard")),
        P(("dp", "shard"), None),
        P(None, ("dp", "shard")),
    )
    out_specs = (
        P(("dp", "shard"), None, None),
        P(("dp", "shard"), None, None),
        P(("dp", "shard"), None, None),
        P(None, ("dp", "shard"), None),
        P(None, ("dp", "shard")),
        P(("dp", "shard"), None),
        P(("dp", "shard")),
        P(("dp", "shard"), None),
        P(None, ("dp", "shard"), None),
        P(None, ("dp", "shard"), None),
        P(None, ("dp", "shard")),
        P(("dp", "shard"), None),
        P(("dp", "shard")),
        P(("dp", "shard"), None),
        P(None, ("dp", "shard")),
    )
    return jax.shard_map(
        per_device, mesh=mesh, in_specs=in_specs, out_specs=out_specs, check_vma=False
    )
```

profile of v0, /device:TPU:14, one launch (start us, length us, event | category | flops | bytes accessed | tf_op | source)
XLA Modules:
  0.0 786.7 jit_solution(3850601012912023010)
XLA Ops:
  25.7 62.4 %all-gather.7.cloned.1.call-done = bf16[128,1,24624]{2,1,0:T(2,128)(2,1)} async-done(((bf16[1,1,24624]{2,1,0:T(2,128)(2,1)}), bf16[128,1,24624]{2,1,0:T(2,128)(2,1)}) %all-gather.7.cloned.1.call-update) | async-done | bytes 6303760 | tf_op jit(solution)/shard_map/all_gather | solution.py:304
  88.2 25.2 %copy.221 = bf16[128,1,24624]{0,2,1:T(8,128)(2,1)} copy(bf16[128,1,24624]{2,1,0:T(2,128)(2,1)} %all-gather.7.cloned.1.call-done) | data formatting | bytes 12607488 | tf_op jit(solution)/shard_map/all_gather | solution.py:304
  114.3 5.2 fusion.176
  159.9 11.8 %all-gather.5.cloned.1.call-done = bf16[128,1,33236]{2,1,0:T(2,128)(2,1)} async-done(((bf16[1,1,33236]{2,1,0:T(2,128)(2,1)}), bf16[128,1,33236]{2,1,0:T(2,128)(2,1)}) %all-gather.5.cloned.1.call-update) | async-done | bytes 8508432 | tf_op jit(solution)/shard_map/all_gather | solution.py:304
  171.7 33.3 %copy.212 = bf16[128,1,33236]{0,2,1:T(8,128)(2,1)} copy(bf16[128,1,33236]{2,1,0:T(2,128)(2,1)} %all-gather.5.cloned.1.call-done) | data formatting | bytes 17016832 | tf_op jit(solution)/shard_map/all_gather | solution.py:304
  206.6 5.8 fusion.175
  224.4 9.1 %fusion.179 = (bf16[1,512,512]{2,0,1:T(2,128)(2,1)}, bf16[1,512,512]{2,0,1:T(2,128)(2,1)}, bf16[1,512,512]{2,0,1:T(2,128)(2,1)S(1)}, bf16[1,512,512]{2,0,1:T(2,128)(2,1)S(1)}) fusion(bf16[4,512,512]{2,0,1:T(4,128)(2,1)} %bitcast.377), kind=kLoop, calls=%fused_computation.351 | loop fusion | bytes 4194304 | tf_op jit(solution)/shard_map/slice | solution.py:83
  252.4 9.0 %fusion.177 = (bf16[1,512,512]{2,0,1:T(2,128)(2,1)}, bf16[1,512,512]{2,0,1:T(2,128)(2,1)}, bf16[1,512,512]{2,0,1:T(2,128)(2,1)}, bf16[1,512,512]{2,0,1:T(2,128)(2,1)S(1)}) fusion(bf16[4,512,512]{2,0,1:T(4,128)(2,1)} %bitcast.378), kind=kLoop, calls=%fused_computation.349 | loop fusion | bytes 4194304 | tf_op jit(solution)/shard_map/slice | solution.py:83
  293.6 4.7 reshape.848
  391.5 4.7 copy.251
  396.2 6.1 reshape.853
  402.8 5.7 reshape.859
  408.6 5.1 reshape.861
  415.9 4.6 copy.253
  420.5 6.3 reshape.862
  426.9 4.7 constant_dynamic-update-slice_fusion.3
  432.0 4.6 copy.254
  436.7 6.1 reshape.863
  443.6 5.6 reshape.871
  449.3 5.0 reshape.873
  461.5 23.0 %dynamic-update-slice.3 = f32[128,33236]{1,0:T(8,128)} dynamic-update-slice(f32[128,33236]{1,0:T(8,128)} %dynamic-update-slice.2, f32[128,8192]{1,0:T(8,128)} %reshape.871, s32[]{} %constant.114, s32[]{} %constant.117) | dynamic-update-slice | bytes 8388612
  486.1 22.4 %dynamic-update-slice.5 = f32[128,33236]{1,0:T(8,128)} dynamic-update-slice(f32[128,33236]{1,0:T(8,128)} %dynamic-update-slice.4, f32[128,8192]{1,0:T(8,128)} %reshape.873, s32[]{} %constant.114, s32[]{} %constant.119) | dynamic-update-slice | bytes 8388612
  510.4 16.1 %concatenate.16 = f32[128,24624]{1,0:T(8,128)} concatenate(f32[128,8192]{1,0:T(8,128)} %reshape.853, f32[128,32]{1,0:T(8,128)S(1)} %reshape.858, f32[128,8192]{1,0:T(8,128)} %reshape.859, f32[128,16]{1,0:T(8,128)S(1)} %reshape.860, f32[128,8192]{1,0:T(8,128)} %reshape.861), dimensions={1} | concatenate | bytes 25214976 | tf_op jit(solution)/shard_map/concatenate | solution.py:260
  532.1 233.5 %all-reduce.5.cloned.1.call-done = (f32[128,24624]{1,0:T(8,128)}, f32[128,33236]{1,0:T(8,128)}) async-done(((f32[128,24624]{1,0:T(8,128)}, f32[128,33236]{1,0:T(8,128)}), (f32[128,24624]{1,0:T(8,128)}, f32[128,33236]{1,0:T(8,128)})) %all-reduce.5.cloned.1.call-update) | async-done | bytes 29624336
  (508 shorter events, 250.9 us)
Async XLA Ops:
  7.2 81.0 %all-gather.7.cloned.1.call-start = ((), (), s32[]{:S(2)}) async-start(), calls=%async_computation.1 | async-start | bytes 12747264 | tf_op jit(solution)/shard_map/all_gather | solution.py:304
  11.9 159.8 %all-gather.5.cloned.1.call-start = ((), (), s32[]{:S(2)}) async-start(), calls=%async_computation | async-start | bytes 17172480 | tf_op jit(solution)/shard_map/all_gather | solution.py:304
  20.3 745.2 %all-reduce.5.cloned.1.call-start = ((), (), s32[]{:S(2)}) async-start(), calls=%async_computation.2 | async-start | bytes 59375616
  23.0 192.2 %copy-start.98 = (s32[384]{0:T(512)}, s32[384]{0:T(512)S(1)}, u32[]{:S(2)}) copy-start(s32[384]{0:T(512)S(1)} %select_reduce_fusion.3) | copy-start | bytes 4612
  25.4 88.0 %copy-start.100 = (f32[384]{0:T(512)}, f32[384]{0:T(512)S(1)}, u32[]{:S(2)}) copy-start(f32[384]{0:T(512)S(1)} %fusion.69) | copy-start | bytes 4612
  25.7 126.8 %copy-start.27 = (pred[384,384]{0,1:T(8,128)(4,1)}, pred[384,384]{0,1:T(8,128)(4,1)S(1)}, u32[]{:S(2)}) copy-start(pred[384,384]{0,1:T(8,128)(4,1)S(1)} %get-tuple-element.158) | copy-start | bytes 442372
  25.7 253.9 %copy-start.29 = (pred[384,384]{0,1:T(8,128)(4,1)}, pred[384,384]{0,1:T(8,128)(4,1)S(1)}, u32[]{:S(2)}) copy-start(pred[384,384]{0,1:T(8,128)(4,1)S(1)} %get-tuple-element.157) | copy-start | bytes 442372
  206.6 8.5 %copy-start.96 = (bf16[1,384,512]{2,1,0:T(8,128)(2,1)S(1)}, bf16[1,384,512]{2,1,0:T(8,128)(2,1)}, u32[]{:S(2)}) copy-start(bf16[1,384,512]{2,1,0:T(8,128)(2,1)} %param.19) | copy-start | bytes 1179652
  215.2 54.8 %copy-start.109 = (f32[512]{0:T(512)}, f32[512]{0:T(512)S(1)}, u32[]{:S(2)}) copy-start(f32[512]{0:T(512)S(1)} %get-tuple-element.103) | copy-start | bytes 6148
  233.8 14.1 %copy-start.18 = (bf16[384,512]{1,0:T(8,128)(2,1)}, bf16[384,512]{1,0:T(8,128)(2,1)S(1)}, u32[]{:S(2)}) copy-start(bf16[384,512]{1,0:T(8,128)(2,1)S(1)} %add_convert_fusion.3) | copy-start | bytes 1179652
  239.9 25.5 %copy-start.35 = (bf16[384,512]{0,1:T(8,128)(2,1)}, bf16[384,512]{0,1:T(8,128)(2,1)S(1)}, u32[]{:S(2)}) copy-start(bf16[384,512]{0,1:T(8,128)(2,1)S(1)} %copy.217) | copy-start | bytes 1179652
  243.6 21.8 %copy-start.33 = (bf16[384,512]{0,1:T(8,128)(2,1)}, bf16[384,512]{0,1:T(8,128)(2,1)S(1)}, u32[]{:S(2)}) copy-start(bf16[384,512]{0,1:T(8,128)(2,1)S(1)} %copy.218) | copy-start | bytes 1179652
  252.4 10.0 %copy-start.67 = (bf16[384,512]{1,0:T(8,128)(2,1)S(1)}, bf16[384,512]{1,0:T(8,128)(2,1)}, u32[]{:S(2)}) copy-start(bf16[384,512]{1,0:T(8,128)(2,1)} %fusion.50) | copy-start | bytes 1179652
  269.9 8.7 %copy-start.104 = (f32[384]{0:T(512)}, f32[384]{0:T(512)S(1)}, u32[]{:S(2)}) copy-start(f32[384]{0:T(512)S(1)} %fusion.143) | copy-start | bytes 4612
  281.0 17.5 %copy-start.69 = (bf16[8,64,384]{2,1,0:T(8,128)(2,1)}, bf16[8,64,384]{2,1,0:T(8,128)(2,1)S(1)}, u32[]{:S(2)}) copy-start(bf16[8,64,384]{2,1,0:T(8,128)(2,1)S(1)} %fusion.43) | copy-start | bytes 1179652
  300.1 7.6 copy-start.6
  327.8 8.1 %slice-start = ((s8[4718592]{0:T(1024)(128)(4,1)}), s8[524288]{0:T(1024)(128)(4,1)S(1)}, s32[]{:S(2)}) async-start(s8[4718592]{0:T(1024)(128)(4,1)} %bitcast.362), calls=%async_computation.3 | async-start | bytes 1048576
  345.7 7.2 slice-start.2
  436.7 6.5 copy-start.108
  436.7 6.5 copy-start.112
  436.7 6.5 copy-start.113
  436.7 6.5 copy-start.120
  436.7 6.5 copy-start.121
  436.7 6.5 copy-start.122
  (114 other events, 370.3 us)
Sparse Core Ops, SparseCore 0:
  12.0 76.0 all-gather.6
  91.7 79.9 all-gather.4
  526.7 238.7 all-reduce.4
where the time goes:
time: 802 us; the launch traced here: 787 us
  local copies, waits for them, and re-layouts  333 us (42%)
  waiting for transfers between devices  308 us (38%)
  matrix products  104 us (13%)
  other arithmetic  25.7 us (3%)
  between operations  15.8 us (2%)
    unnamed x4, waiting for transfers between devices  234 us
    unnamed x289, local copies, waits for them, and re-layouts  76.6 us
    all_gather x2, waiting for transfers between devices, collect(): gathered = lax.all_gather(packed, ('dp', 'shard'), axis=0, tiled=True)  74.3 us
    all_gather x2, local copies, waits for them, and re-layouts, collect(): gathered = lax.all_gather(packed, ('dp', 'shard'), axis=0, tiled=True)  58.5 us
    reshape x12, local copies, waits for them, and re-layouts, pack_rows(): pieces.append(moved.reshape(count, -1))  40.3 us
    slice x15, local copies, waits for them, and re-layouts, unpack_full(): gathered[:, offset:offset + amount]  39.4 us
    dot_general x16, matrix products, outer_sum(): lax.dot_general(left, right, (((0,), (0,)), ((), ())), preferred_element_...  27.7 us
    reshape x10, local copies, waits for them, and re-layouts, unpack_full(): gathered[:, offset:offset + amount]  27 us
  transfers between devices with their start and end apart: 3, of which 3 were waited for; matrix products, arithmetic and copies ran while one was open for 11% of the time, Pallas kernels for 0%

commit v1 on v0

v1 whole, which is shorter than its diff:
```python
import functools
import itertools

import jax
import jax.numpy as jnp
from jax import lax
from jax.experimental import pallas as pl
from jax.experimental.pallas import tpu as pltpu
from jax.sharding import Mesh
from jax.sharding import PartitionSpec as P

D = 512
HEADS = 8
HEAD_DIM = 64
FF = 2048
LANGS = 100
SEQ = 384
DOCS = 5
EPSILON = 1e-05
NEGATIVE = -1000000000.0
OPEN = 3e38
SCALE = HEAD_DIM ** (-0.5)
AXES = ("x", "c", "y", "z")
SIZES = (4, 2, 4, 4)
BLOCKS = 32
ENC_VEC = 104
DEC_VEC = 112
CHUNK = 128
CHUNKS = SEQ // CHUNK
F32 = jnp.float32
BF16 = jnp.bfloat16


def dot(left, right):
    return lax.dot_general(left, right, (((1,), (0,)), ((), ())), preferred_element_type=F32)


def dot_nt(left, right):
    return lax.dot_general(left, right, (((1,), (1,)), ((), ())), preferred_element_type=F32)


def rows(index, size=CHUNK):
    return slice(index * size, (index + 1) * size)


def normed(values):
    mean = jnp.mean(values, axis=-1, keepdims=True)
    center = values - mean
    rstd = lax.rsqrt(jnp.mean(center * center, axis=-1, keepdims=True) + EPSILON)
    return center * rstd, rstd


def layer_norm(source, gain, shift, out):
    for i in range(CHUNKS):
        hat, _ = normed(source[rows(i), :])
        out[rows(i), :] = (hat * gain + shift).astype(BF16)


def norm_back(source, gain, grad, base, out):
    d_gain = jnp.zeros((1, D), F32)
    d_shift = jnp.zeros((1, D), F32)
    for i in range(CHUNKS):
        hat, rstd = normed(source[rows(i), :])
        dy = grad[rows(i), :]
        d_gain = d_gain + jnp.sum(dy * hat, axis=0, keepdims=True)
        d_shift = d_shift + jnp.sum(dy, axis=0, keepdims=True)
        dyg = dy * gain
        mean_one = jnp.mean(dyg, axis=-1, keepdims=True)
        mean_two = jnp.mean(dyg * hat, axis=-1, keepdims=True)
        out[rows(i), :] = base[rows(i), :].astype(F32) + rstd * (dyg - mean_one - hat * mean_two)
    return d_gain, d_shift


def low_lanes(count):
    return lax.broadcasted_iota(jnp.int32, (count, 128), 1) < HEAD_DIM


def head_mask():
    lane = lax.broadcasted_iota(jnp.int32, (1, D), 1)
    return ((lane // HEAD_DIM) % 2 == 0).astype(F32)


def doc_ids(lengths, shape, axis):
    position = lax.broadcasted_iota(jnp.int32, shape, axis)
    total = jnp.zeros(shape, jnp.int32)
    end = 0
    for i in range(DOCS):
        end = end + lengths[0, i]
        total = total + (position >= end).astype(jnp.int32)
    return total


def masks(s_len, t_len, bias_e, bias_s, bias_c):
    shape = (SEQ, SEQ)
    s_row = doc_ids(s_len, (1, SEQ), 1)
    t_row = doc_ids(t_len, (1, SEQ), 1)
    s_col = doc_ids(s_len, (SEQ, 1), 0)
    t_col = doc_ids(t_len, (SEQ, 1), 0)
    for i in range(CHUNKS):
        shape = (CHUNK, SEQ)
        sc = jnp.broadcast_to(s_col[rows(i), :], shape)
        tc = jnp.broadcast_to(t_col[rows(i), :], shape)
        key = lax.broadcasted_iota(jnp.int32, shape, 1)
        query = lax.broadcasted_iota(jnp.int32, shape, 0) + i * CHUNK
        bias_e[rows(i), :] = jnp.where(sc == s_row, OPEN, NEGATIVE)
        bias_s[rows(i), :] = jnp.where((tc == t_row) & (key <= query), OPEN, NEGATIVE)
        bias_c[rows(i), :] = jnp.where(tc == s_row, OPEN, NEGATIVE)


def lang_onehot(t_len, langs):
    doc = doc_ids(t_len, (SEQ, 128), 0)
    lang = jnp.zeros((SEQ, 128), jnp.int32)
    for i in range(DOCS):
        lang = jnp.where(doc == i, langs[0, i], lang)
    lane = lax.broadcasted_iota(jnp.int32, (SEQ, 128), 1)
    return jnp.where(lang == lane, 1.0, 0.0).astype(BF16)


def attn_project(query_in, memory, weights, bias_q, bias_v, q_even, q_odd, keys, values):
    even = head_mask()
    for i in range(CHUNKS):
        u = query_in[rows(i), :]
        m = memory[rows(i), :]
        q = SCALE * (dot(u, weights[0]) + bias_q)
        q_even[rows(i), :] = (q * even).astype(BF16)
        q_odd[rows(i), :] = (q * (1.0 - even)).astype(BF16)
        keys[rows(i), :] = dot(m, weights[1]).astype(BF16)
        values[rows(i), :] = (dot(m, weights[2]) + bias_v).astype(BF16)


def attn_core(q_even, q_odd, keys, values, bias, probs, context, causal):
    low = low_lanes(CHUNK)
    for pair in range(HEADS // 2):
        lanes = rows(pair, 128)
        for i in range(CHUNKS):
            limit = (i + 1) * CHUNK if causal else SEQ
            parts = []
            for half, query in enumerate((q_even, q_odd)):
                s = dot_nt(query[rows(i), lanes], keys[:limit, lanes])
                s = jnp.minimum(s, bias[rows(i), :limit])
                e = jnp.exp(s - jnp.max(s, axis=-1, keepdims=True))
                p = (e * (1.0 / jnp.sum(e, axis=-1, keepdims=True))).astype(BF16)
                probs[2 * pair + half, rows(i), :limit] = p
                parts.append(dot(p, values[:limit, lanes]))
            context[rows(i), lanes] = jnp.where(low, parts[0], parts[1]).astype(BF16)


def attn_output(context, weight, bias_o, residual, out):
    for i in range(CHUNKS):
        branch = dot(context[rows(i), :], weight[...]) + bias_o
        out[rows(i), :] = residual[rows(i), :].astype(F32) + branch


def put_rows(out, table, unit, first, value):
    for j in range(value.shape[0] // 16):
        out[table[first + j], unit] = value[rows(j, 16), :].astype(BF16)


def weight_grad(left_t, right, out, table, unit, scale=None):
    for i in range(D // CHUNK):
        value = dot(left_t[rows(i), :], right[...])
        if scale is not None:
            value = value * scale
        put_rows(out, table, unit, i * (CHUNK // 16), value)


def column_sum(ref):
    return jnp.sum(ref[...].astype(F32), axis=0, keepdims=True)


def attn_back(grad, query_in_t, memory_t, weights, kept, scratch, out, table, unit, causal):
    q_even, q_odd, keys, values, probs, context = kept
    d_even, d_odd, dc_t, q_t, c_t, ds, dq, dk_t, dv_t, dk, dv, du, dm = scratch
    even = head_mask()
    for i in range(CHUNKS):
        dc = dot_nt(grad[rows(i), :], weights[3])
        d_even[rows(i), :] = (dc * even).astype(BF16)
        d_odd[rows(i), :] = (dc * (1.0 - even)).astype(BF16)
    dc_t[...] = (d_even[...] + d_odd[...]).T
    q_t[...] = (q_even[...] + q_odd[...]).T
    c_t[...] = context[...].T
    low = low_lanes(CHUNK)
    for pair in range(HEADS // 2):
        lanes = rows(pair, 128)
        parts = []
        for half, d_ctx in enumerate((d_even, d_odd)):
            head = 2 * pair + half
            pieces = []
            for i in range(CHUNKS):
                limit = (i + 1) * CHUNK if causal else SEQ
                dch = d_ctx[rows(i), lanes]
                total = jnp.sum(
                    dch.astype(F32) * context[rows(i), lanes].astype(F32), axis=-1, keepdims=True
                )
                dp = dot_nt(dch, values[:limit, lanes])
                p = probs[head, rows(i), :limit].astype(F32)
                d_score = (p * (dp - total)).astype(BF16)
                ds[rows(i), :limit] = d_score
                pieces.append(dot(d_score, keys[:limit, lanes]))
            parts.append(pieces)
            span = rows(head, HEAD_DIM)
            if causal:
                for j in range(CHUNKS):
                    start = j * CHUNK
                    dk_t[span, rows(j)] = dot(q_t[span, start:], ds[start:, rows(j)]).astype(BF16)
                    dv_t[span, rows(j)] = dot(
                        dc_t[span, start:], probs[head, start:, rows(j)]
                    ).astype(BF16)
            else:
                dk_t[span, :] = dot(q_t[span, :], ds[...]).astype(BF16)
                dv_t[span, :] = dot(dc_t[span, :], probs[head]).astype(BF16)
        for i in range(CHUNKS):
            dq[rows(i), lanes] = jnp.where(low, parts[0][i], parts[1][i]).astype(BF16)
    dk[...] = dk_t[...].T
    dv[...] = dv_t[...].T
    weight_grad(query_in_t, dq, out, table, unit, SCALE)
    weight_grad(memory_t, dk, out, table, unit + 1)
    weight_grad(memory_t, dv, out, table, unit + 2)
    weight_grad(c_t, grad, out, table, unit + 3)
    for i in range(CHUNKS):
        du[rows(i), :] = SCALE * dot_nt(dq[rows(i), :], weights[0])
        dm[rows(i), :] = dot_nt(dk[rows(i), :], weights[1]) + dot_nt(dv[rows(i), :], weights[2])
    return SCALE * column_sum(dq), column_sum(dv), column_sum(grad)


def silu_parts(hidden):
    gate = 1.0 / (1.0 + jnp.exp(-hidden))
    return hidden * gate, gate


def feed_forward(inputs, w_in, b_in, w_out, bias, residual, out):
    for i in range(CHUNKS):
        u = inputs[rows(i), :]
        total = residual[rows(i), :] + bias
        for k in range(FF // D):
            hidden = dot(u, w_in[k]) + b_in[:, rows(k, D)]
            active, _ = silu_parts(hidden)
            total = total + dot(active.astype(BF16), w_out[k])
        out[rows(i), :] = total


def feed_both(
    inputs, inputs_t, w_in, b_in, w_out, grad, act, dh, total, d_in, out, table, unit_in, wout_out, b_grad
):
    for k in range(FF // D):
        for i in range(CHUNKS):
            hidden = dot(inputs[rows(i), :], w_in[k]) + b_in[:, rows(k, D)]
            active, gate = silu_parts(hidden)
            low = active.astype(BF16)
            act[rows(i), :] = low
            d_act = dot_nt(grad[rows(i), :], w_out[k])
            dh[rows(i), :] = (d_act * (gate + active * (1.0 - gate))).astype(BF16)
            if total is not None:
                total[rows(i), :] = total[rows(i), :] + dot(low, w_out[k])
            back = dot_nt(dh[rows(i), :], w_in[k])
            d_in[rows(i), :] = back if k == 0 else d_in[rows(i), :] + back
        b_grad[:, rows(k, D)] = column_sum(dh)
        weight_grad(inputs_t, dh, out, table, unit_in + k)
        act_t = act[...].T
        for i in range(D // CHUNK):
            value = dot(act_t[rows(i), :], grad[...])
            for j in range(CHUNK // 64):
                block = k * 8 + i * 2 + j
                for z in range(4):
                    start = j * 64 + z * 16
                    wout_out[table[block], z] = value[start : start + 16, :].astype(BF16)


def load(source, table, jobs, sem):
    def step(block, carry):
        slot = table[block]
        for k, (unit, target) in enumerate(jobs):
            if len(target.shape) == 3:
                place = target.at[:, pl.ds(pl.multiple_of(block * 16, 16), 16), :]
            else:
                place = target.at[block]
            pltpu.make_async_copy(source.at[slot, pl.ds(unit, 4)], place, sem.at[k]).start()
        return carry

    lax.fori_loop(0, BLOCKS, step, 0)


def arrived(target, sem):
    pltpu.make_async_copy(target, target, sem).wait()


class Wide:
    def __init__(self, ref):
        self.ref = ref

    def __getitem__(self, k):
        return self.ref[8 * k : 8 * k + 8].reshape(D, D)


def first_kernel(
    tab_a, tab_b, s_len, t_len, langs, source, target, cot, vecs, b_enc, b_dec, ga, gb,
    dec_out, d_ffn, g_second, g_rows, g_bias,
    e_n, e_qe, e_qo, e_k, e_v, e_p, e_c, e_mid, e_n2, memory,
    start, s_n, s_qe, s_qo, s_k, s_v, s_p, s_c, first, c_n, c_qe, c_qo, c_k, c_v, c_p, c_c,
    we, wi, wo, ws, wc, vi, vo, bias_e, bias_s, bias_c, buf, second, n3, n3_t, act, dh, d_in, sem_a, sem_b,
):
    load(ga, tab_a, ((0, we), (4, wi), (8, wo)), sem_a)
    load(gb, tab_b, ((0, ws), (4, wc), (8, vi), (12, vo)), sem_b)
    masks(s_len, t_len, bias_e, bias_s, bias_c)

    def vec(index):
        return vecs[index : index + 1, :]

    def enc(index):
        return vec(ENC_VEC + index)

    def dec(index):
        return vec(DEC_VEC + index)

    onehot = lang_onehot(t_len, langs)
    table = vecs[...].astype(BF16)
    for i in range(CHUNKS):
        buf[rows(i), :] = source[rows(i), :].astype(F32)
        start[rows(i), :] = target[rows(i), :].astype(F32) + dot(onehot[rows(i), :], table)
    layer_norm(buf, enc(0), enc(1), e_n)
    layer_norm(start, dec(0), dec(1), s_n)
    arrived(we, sem_a.at[0])
    attn_project(e_n, e_n, we, enc(2), enc(3), e_qe, e_qo, e_k, e_v)
    attn_core(e_qe, e_qo, e_k, e_v, bias_e, e_p, e_c, False)
    attn_output(e_c, we.at[3], enc(4), source, e_mid)
    layer_norm(e_mid, enc(5), enc(6), e_n2)
    arrived(wi, sem_a.at[1])
    arrived(wo, sem_a.at[2])
    feed_forward(e_n2, wi, b_enc, Wide(wo), enc(7), e_mid, buf)
    for i in range(CHUNKS):
        memory[rows(i), :] = buf[rows(i), :].astype(BF16)
    arrived(ws, sem_b.at[0])
    attn_project(s_n, s_n, ws, dec(2), dec(3), s_qe, s_qo, s_k, s_v)
    attn_core(s_qe, s_qo, s_k, s_v, bias_s, s_p, s_c, True)
    attn_output(s_c, ws.at[3], dec(4), start, first)
    layer_norm(first, dec(5), dec(6), c_n)
    arrived(wc, sem_b.at[1])
    attn_project(c_n, memory, wc, dec(7), dec(8), c_qe, c_qo, c_k, c_v)
    attn_core(c_qe, c_qo, c_k, c_v, bias_c, c_p, c_c, False)
    attn_output(c_c, wc.at[3], dec(9), first, second)
    layer_norm(second, dec(10), dec(11), n3)
    n3_t[...] = n3[...].T
    arrived(vi, sem_b.at[2])
    arrived(vo, sem_b.at[3])
    for i in range(CHUNKS):
        buf[rows(i), :] = second[rows(i), :] + dec(12)
    feed_both(
        n3, n3_t, vi, b_dec, Wide(vo), cot, act, dh, buf, d_in,
        d_ffn, tab_b, 0, d_ffn.at[:, 4:8], g_bias,
    )
    for i in range(CHUNKS):
        dec_out[rows(i), :] = buf[rows(i), :].astype(BF16)
    d_gain, d_shift = norm_back(second, dec(10), d_in, cot, g_second)
    g_rows[...] = jnp.zeros(g_rows.shape, F32)
    g_rows[0:1, :] = d_gain
    g_rows[1:2, :] = d_shift
    g_rows[2:3, :] = column_sum(cot)


def second_kernel(
    tab_b, t_len, langs, vecs, g_second, g_rows, memory,
    start, s_n, s_qe, s_qo, s_k, s_v, s_p, s_c, first, c_n, c_qe, c_qo, c_k, c_v, c_p, c_c, gb,
    d_attn, g_start, g_memory, g_vec,
    ws, wc, low, u_t, m_t, g_first, d_even, d_odd, dc_t, q_t, c_t, ds, dq, dk_t, dv_t, dk, dv, du, dm, sem,
):
    load(gb, tab_b, ((0, ws), (4, wc)), sem)
    scratch = (d_even, d_odd, dc_t, q_t, c_t, ds, dq, dk_t, dv_t, dk, dv, du, dm)

    def dec(index):
        return vecs[DEC_VEC + index : DEC_VEC + index + 1, :]

    u_t[...] = c_n[...].T
    m_t[...] = memory[...].T
    low[...] = g_second[...].astype(BF16)
    arrived(ws, sem.at[0])
    arrived(wc, sem.at[1])
    bias_two = attn_back(
        low, u_t, m_t, wc, (c_qe, c_qo, c_k, c_v, c_p, c_c), scratch, d_attn, tab_b, 4, False
    )
    g_memory[...] = dm[...]
    gain_two = norm_back(first, dec(5), du, g_second, g_first)
    low[...] = g_first[...].astype(BF16)
    u_t[...] = s_n[...].T
    bias_one = attn_back(
        low, u_t, u_t, ws, (s_qe, s_qo, s_k, s_v, s_p, s_c), scratch, d_attn, tab_b, 0, True
    )
    du[...] = du[...] + dm[...]
    gain_one = norm_back(start, dec(0), du, g_first, g_start)
    onehot = lang_onehot(t_len, langs)
    g_vec[...] = lax.dot_general(
        onehot, g_start[...].astype(BF16), (((0,), (0,)), ((), ())), preferred_element_type=F32
    )
    values = gain_one + bias_one + gain_two + bias_two
    for i, value in enumerate(values):
        g_vec[DEC_VEC + i : DEC_VEC + i + 1, :] = value
    g_vec[DEC_VEC + 10 : DEC_VEC + 13, :] = g_rows[0:3, :]


def third_kernel(
    tab_a, vecs, b_enc, source, g_memory, g_vec, g_bias,
    e_n, e_qe, e_qo, e_k, e_v, e_p, e_c, e_mid, e_n2, ga,
    d_enc, g_source,
    we, wi, wo, buf, low, u_t, act, dh, d_in, g_mid, b_grad, all_vec,
    d_even, d_odd, dc_t, q_t, c_t, ds, dq, dk_t, dv_t, dk, dv, du, dm, sem,
):
    load(ga, tab_a, ((0, we), (4, wi), (8, wo)), sem)
    scratch = (d_even, d_odd, dc_t, q_t, c_t, ds, dq, dk_t, dv_t, dk, dv, du, dm)

    def enc(index):
        return vecs[ENC_VEC + index : ENC_VEC + index + 1, :]

    u_t[...] = e_n2[...].T
    low[...] = g_memory[...].astype(BF16)
    arrived(wi, sem.at[1])
    arrived(wo, sem.at[2])
    feed_both(
        e_n2, u_t, wi, b_enc, Wide(wo), low, act, dh, None, d_in,
        d_enc, tab_a, 4, d_enc.at[:, 8:12], b_grad,
    )
    bias_out = column_sum(low)
    gain_two = norm_back(e_mid, enc(5), d_in, g_memory, g_mid)
    low[...] = g_mid[...].astype(BF16)
    u_t[...] = e_n[...].T
    arrived(we, sem.at[0])
    bias_one = attn_back(
        low, u_t, u_t, we, (e_qe, e_qo, e_k, e_v, e_p, e_c), scratch, d_enc, tab_a, 0, False
    )
    du[...] = du[...] + dm[...]
    for i in range(CHUNKS):
        buf[rows(i), :] = source[rows(i), :].astype(F32)
    gain_one = norm_back(buf, enc(0), du, g_mid, g_source)
    all_vec[...] = g_vec[...]
    for i, value in enumerate(gain_one + bias_one + gain_two + (bias_out,)):
        all_vec[ENC_VEC + i : ENC_VEC + i + 1, :] = value
    turned = all_vec[...].T.astype(BF16)
    zero = jnp.zeros((16, 128), BF16)
    for block in range(BLOCKS):
        slot = tab_a[block]
        tile = rows(block // 2, 128)
        d_enc[slot, 12, :, 0:128] = turned[rows(block, 16), :]
        d_enc[slot, 12, :, 128:256] = jnp.broadcast_to(b_grad[:, tile], (16, 128)).astype(BF16)
        d_enc[slot, 12, :, 256:384] = jnp.broadcast_to(g_bias[:, tile], (16, 128)).astype(BF16)
        d_enc[slot, 12, :, 384:512] = zero


VM = pl.BlockSpec(memory_space=pltpu.VMEM)
SM = pl.BlockSpec(memory_space=pltpu.SMEM)
HB = pl.BlockSpec(memory_space=pl.ANY)


def act_shape(dtype=BF16):
    return ((SEQ, D), dtype)


KEPT = [act_shape()] * 5 + [((HEADS, SEQ, SEQ), BF16), act_shape()]


def call(body, in_specs, outs, scratch, flops, args):
    return pl.pallas_call(
        body,
        in_specs=in_specs,
        out_specs=[VM] * len(outs),
        out_shape=[jax.ShapeDtypeStruct(s, t) for s, t in outs],
        scratch_shapes=[
            pltpu.VMEM(*s) if isinstance(s, tuple) else pltpu.SemaphoreType.DMA((s,))
            for s in scratch
        ],
        compiler_params=pltpu.CompilerParams(vmem_limit_bytes=63 * 1024 * 1024),
        cost_estimate=pl.CostEstimate(flops=flops, bytes_accessed=1 << 24, transcendentals=0),
    )(*args)


SQUARE = ((4, D, D), BF16)
TALL = ((BLOCKS, 4, 16, D), BF16)
TURN = ((D, SEQ), BF16)
BIAS = ((SEQ, SEQ), F32)
BACK = [act_shape()] * 2 + [TURN] * 3 + [((SEQ, SEQ), BF16), act_shape(), TURN, TURN, act_shape(), act_shape()]
BACK = BACK + [act_shape(F32)] * 2


def pairs(axis, step):
    k = AXES.index(axis)
    found = []

    def flat(place):
        index = 0
        for at, size in zip(place, SIZES):
            index = index * size + at
        return index

    for place in itertools.product(*[range(size) for size in SIZES]):
        if axis == "c":
            other = 1
        else:
            other = 1 if (step == 0) == (place[1] == 0) else 3
        target = list(place)
        target[k] = place[k] ^ other
        found.append((flat(place), flat(target)))
    return found


def swap(values, axis, step=0):
    return lax.ppermute(values, AXES, pairs(axis, step))


def slot_of(distance, core):
    zero = jnp.array([0, 1, 3, 2], jnp.int32)[distance]
    one = jnp.array([0, 2, 3, 1], jnp.int32)[distance]
    return jnp.where(core == 0, zero, one)


def slot_table(inner, outer):
    block = jnp.arange(BLOCKS, dtype=jnp.int32)
    at = {"x": block // 8, "c": (block // 4) % 2, "y": block % 4}
    me = {name: lax.axis_index(name) for name in AXES}
    core = at["c"]
    other = (core != me["c"]).astype(jnp.int32)
    return (
        16 * other
        + slot_of(at[inner] ^ me[inner], core)
        + 4 * slot_of(at[outer] ^ me[outer], core)
    )


def z_order(values, axis):
    me = lax.axis_index("z")
    core = lax.axis_index("c")
    picks = [lax.dynamic_index_in_dim(values, slot_of(q ^ me, core), axis) for q in range(4)]
    return jnp.concatenate(picks, axis)


def z_slots(values, axis):
    me = lax.axis_index("z")
    hop = jnp.where(lax.axis_index("c") == 0, 1, 3)
    picks = [lax.dynamic_index_in_dim(values, me ^ q, axis) for q in (0, hop, 4 - hop, 2)]
    return jnp.concatenate(picks, axis)


def grow(values, axis):
    for step in range(2):
        values = jnp.concatenate([values, swap(values, axis, step)], axis=0)
    return values


def shrink(values, axis, last=BF16):
    for step in (1, 0):
        half = values.shape[0] // 2
        received = swap(values[half:], axis, step)
        total = values[:half].astype(F32) + received.astype(F32)
        values = total.astype(BF16 if step else last)
    return values


def gather(units):
    around = z_order(grow(units[None], "z"), 0)

    def merge(first, last):
        part = around[:, first:last].reshape(4, last - first, 4, 4, D)
        return part.transpose(1, 2, 0, 3, 4).reshape((last - first) * 4, 16, D)

    enc = jnp.concatenate([merge(0, 2), around[:, 2]], axis=0)[None]
    dec = jnp.concatenate([merge(3, 6), around[:, 6]], axis=0)[None]
    enc = grow(grow(enc, "x"), "y")
    dec = grow(grow(dec, "y"), "x")
    return (
        jnp.concatenate([enc, swap(enc, "c")], axis=0),
        jnp.concatenate([dec, swap(dec, "c")], axis=0),
    )


def scatter(grads, inner, outer, wide):
    received = swap(grads[16:], "c")
    values = (grads[:16].astype(F32) + received.astype(F32)).astype(BF16)
    values = shrink(shrink(values, outer), inner)[0]
    narrow = values
    if wide is not None:
        narrow = jnp.concatenate([values[: wide[0]], values[wide[1] :]], axis=0)
    count = narrow.shape[0]
    parts = narrow.reshape(count, 4, 4, D).transpose(1, 0, 2, 3).reshape(4, count * 4, D)
    if wide is not None:
        parts = jnp.concatenate([parts, values[wide[0] : wide[1]]], axis=1)
    total = shrink(z_slots(parts, 0), "z", F32)[0]
    return total[: count * 4].reshape(count, 4, D), total[count * 4 :]


def turn_in(shard):
    return shard.reshape(4, 4, D).transpose(1, 0, 2).reshape(16, D)


def per_device(
    source, target, source_lengths, target_lengths, lang_ids, out_cotangent,
    enc_attn, enc_vectors, enc_w_in, enc_b_in, enc_w_out,
    dec_self, dec_cross, dec_vectors, dec_w_in, dec_b_in, dec_w_out, lang_table,
):
    small = jnp.concatenate(
        [
            lang_table.T,
            jnp.zeros((4, ENC_VEC - LANGS), BF16),
            enc_vectors.T,
            dec_vectors.T,
            jnp.zeros((4, 128 - DEC_VEC - 13), BF16),
            enc_b_in.reshape(4, 4),
            dec_b_in.reshape(4, 4),
            jnp.zeros((4, 120), BF16),
        ],
        axis=1,
    )
    small = lax.all_gather(small, AXES, axis=0, tiled=True)
    vecs = small[:, :128].T.astype(F32)
    b_enc = small[:, 128:132].reshape(1, FF).astype(F32)
    b_dec = small[:, 132:136].reshape(1, FF).astype(F32)
    units = jnp.stack(
        [
            enc_attn.reshape(16, D),
            turn_in(enc_w_in),
            enc_w_out,
            dec_self.reshape(16, D),
            dec_cross.reshape(16, D),
            turn_in(dec_w_in),
            dec_w_out,
        ]
    )
    ga, gb = gather(units)
    tab_a = slot_table("x", "y")
    tab_b = slot_table("y", "x")

    (
        dec_out, d_ffn, g_second, g_rows, g_bias,
        *rest,
    ) = call(
        first_kernel,
        [SM] * 5 + [VM] * 6 + [HB] * 2,
        [act_shape(), ((BLOCKS, 8, 16, D), BF16), act_shape(F32), ((8, D), F32), ((1, FF), F32)]
        + KEPT
        + [act_shape(F32), act_shape(), act_shape()]
        + [act_shape(F32)]
        + KEPT
        + [act_shape(F32)]
        + KEPT,
        [SQUARE, SQUARE, TALL, SQUARE, SQUARE, SQUARE, TALL, BIAS, BIAS, BIAS]
        + [act_shape(F32), act_shape(F32), act_shape(), TURN, act_shape(), act_shape(), act_shape(F32), 3, 4],
        12 * 10**9,
        (
            tab_a, tab_b, source_lengths, target_lengths, lang_ids,
            source[0], target[0], out_cotangent[0], vecs, b_enc, b_dec, ga, gb,
        ),
    )
    enc_kept, memory, dec_kept = rest[:9], rest[9], rest[10:]
    ffn_small, ffn_tall = scatter(d_ffn, "y", "x", (4, 8))
    d_attn, g_start, g_memory, g_vec = call(
        second_kernel,
        [SM] * 3 + [VM] * 20 + [HB],
        [((BLOCKS, 8, 16, D), BF16), act_shape(F32), act_shape(F32), ((128, D), F32)],
        [SQUARE, SQUARE, act_shape(), TURN, TURN, act_shape(F32)] + BACK + [2],
        6 * 10**9,
        (tab_b, target_lengths, lang_ids, vecs, g_second, g_rows, memory, *dec_kept, gb),
    )
    attn_small, _ = scatter(d_attn, "y", "x", None)
    d_enc, g_source = call(
        third_kernel,
        [SM] + [VM] * 15 + [HB],
        [((BLOCKS, 13, 16, D), BF16), act_shape(F32)],
        [SQUARE, SQUARE, TALL, act_shape(F32), act_shape(), TURN, act_shape(), act_shape()]
        + [act_shape(F32), act_shape(F32), ((1, FF), F32), ((128, D), F32)]
        + BACK
        + [3],
        8 * 10**9,
        (tab_a, vecs, b_enc, source[0], g_memory, g_vec, g_bias, *enc_kept, ga),
    )
    enc_small, enc_tall = scatter(d_enc, "x", "y", (8, 12))
    last = enc_small[8]
    offset = (lax.axis_index("y") % 2) * 64 + lax.axis_index("z") * 16
    bias_enc = lax.dynamic_slice(last, (0, 128 + offset), (1, 16)).reshape(16)
    bias_dec = lax.dynamic_slice(last, (0, 256 + offset), (1, 16)).reshape(16)
    vec_grads = last[:, :128].T

    def turn_out(part):
        return part.transpose(1, 0, 2).reshape(4, FF)

    return (
        dec_out[None],
        g_source[None],
        g_start[None],
        enc_small[0:4],
        vec_grads[ENC_VEC : ENC_VEC + 8],
        turn_out(enc_small[4:8]),
        bias_enc,
        enc_tall,
        attn_small[0:4],
        attn_small[4:8],
        vec_grads[DEC_VEC : DEC_VEC + 13],
        turn_out(ffn_small[0:4]),
        bias_dec,
        ffn_tall,
        vec_grads[:LANGS],
    )


def solution(mesh):
    fine = Mesh(mesh.devices.reshape(SIZES), AXES)
    flat = AXES
    in_specs = (
        P(flat, None, None),
        P(flat, None, None),
        P(flat, None),
        P(flat, None),
        P(flat, None),
        P(flat, None, None),
        P(None, flat, None),
        P(None, flat),
        P(flat, None),
        P(flat),
        P(flat, None),
        P(None, flat, None),
        P(None, flat, None),
        P(None, flat),
        P(flat, None),
        P(flat),
        P(flat, None),
        P(None, flat),
    )
    out_specs = (
        P(flat, None, None),
        P(flat, None, None),
        P(flat, None, None),
        P(None, flat, None),
        P(None, flat),
        P(flat, None),
        P(flat),
        P(flat, None),
        P(None, flat, None),
        P(None, flat, None),
        P(None, flat),
        P(flat, None),
        P(flat),
        P(flat, None),
        P(None, flat),
    )
    return jax.shard_map(
        per_device, mesh=fine, in_specs=in_specs, out_specs=out_specs, check_vma=False
    )
```

time: 802 us -> 430 us (0.54); the launches traced: 787 us -> 423 us
  local copies, waits for them, and re-layouts: 333 us -> 54.8 us
  waiting for transfers between devices: 308 us -> 144 us
  matrix products: 104 us -> 0 us
  Pallas kernels: 0 us -> 102 us
  blocking collectives: 0 us -> 57.6 us
  starting transfers between devices: 0.12 us -> 36.2 us
  between operations: 15.8 us -> 6.93 us
    unnamed x4 -> x0, waiting for transfers between devices: 234 us -> none
    ppermute x0 -> x33, waiting for transfers between devices: none -> 144 us  [swap(): return lax.ppermute(values, AXES, pairs(axis, step))]
    dot_general x68 -> x0, matrix products: 104 us -> none  [the longest x16 27.7 us: outer_sum(): lax.dot_general(left, right, (((0,), (0,)), ((), ())), preferred_element_...]
    pallas_call x0 -> x3, Pallas kernels: none -> 102 us  [call(): pl.pallas_call(body, in_specs=in_specs, out_specs=[VM] * len(outs), out_s...]
    all_gather x2 -> x0, waiting for transfers between devices: 74.3 us -> none  [collect(): gathered = lax.all_gather(packed, ('dp', 'shard'), axis=0, tiled=True)]
    reshape x28 -> x11, local copies, waits for them, and re-layouts: 69.7 us -> 1.64 us  [the longest x1 0.63 us: scatter(): return (total[:count * 4].reshape(count, 4, D), total[count * 4:])]
    unnamed x289 -> x52, local copies, waits for them, and re-layouts: 76.6 us -> 14.2 us
    all_gather x2 -> x0, local copies, waits for them, and re-layouts: 58.5 us -> none  [collect(): gathered = lax.all_gather(packed, ('dp', 'shard'), axis=0, tiled=True)]
  transfers between devices with their start and end apart: 3 -> 33, of which waited for: 3 -> 19; matrix products, arithmetic and copies ran while one was open for 11% -> 12% of each run, Pallas kernels for 0% -> 12%
where the time goes in v1:
time: 430 us; the launch traced here: 423 us
  waiting for transfers between devices  144 us (33%)
  Pallas kernels  102 us (24%)
  blocking collectives  57.6 us (13%)
  local copies, waits for them, and re-layouts  54.8 us (13%)
  starting transfers between devices  36.2 us (8%)
  other arithmetic  22.8 us (5%)
  between operations  6.93 us (2%)
    ppermute x33, waiting for transfers between devices, swap(): return lax.ppermute(values, AXES, pairs(axis, step))  144 us
    pallas_call x3, Pallas kernels, call(): pl.pallas_call(body, in_specs=in_specs, out_specs=[VM] * len(outs), out_s...  102 us
    all_gather x1, blocking collectives, per_device(): small = lax.all_gather(small, AXES, axis=0, tiled=True)  57.6 us
    ppermute x33, starting transfers between devices, swap(): return lax.ppermute(values, AXES, pairs(axis, step))  36.2 us
    unnamed x52, local copies, waits for them, and re-layouts  14.2 us
    slice x3, local copies, waits for them, and re-layouts, scatter(): received = swap(grads[16:], 'c')  8.86 us
    convert_element_type x15, other arithmetic, shrink(): values = total.astype(BF16 if step else last)  8.8 us
  transfers between devices with their start and end apart: 33, of which 19 were waited for; matrix products, arithmetic and copies ran while one was open for 12% of the time, Pallas kernels for 12%

profile of v1, /device:TPU:14, one launch (start us, length us, event | category | flops | bytes accessed | tf_op | source)
XLA Modules:
  0.0 423.5 jit_solution(13021478354206340144)
XLA Ops:
  10.6 4.1 collective-permute-start.1
  22.3 7.3 %collective-permute-done.7 = bf16[1,16,16,512]{3,2,1,0:T(8,128)(2,1)S(1)} collective-permute-done((bf16[1,16,16,512]{3,2,1,0:T(8,128)(2,1)S(1)}, bf16[1,16,16,512]{3,2,1,0:T(8,128)(2,1)S(1)}, u32[]{:S(2)}, u32[]{:S(2)}) %collective-permute-start.7) | collective-permute-done | bytes 262176 | tf_op jit(solution)/shard_map/ppermute | solution.py:503
  30.6 8.4 %collective-permute-done.8 = bf16[2,16,16,512]{3,2,1,0:T(8,128)(2,1)S(1)} collective-permute-done((bf16[2,16,16,512]{3,2,1,0:T(8,128)(2,1)S(1)}, bf16[2,16,16,512]{3,2,1,0:T(8,128)(2,1)S(1)}, u32[]{:S(2)}, u32[]{:S(2)}) %collective-permute-start.8) | collective-permute-done | bytes 524320 | tf_op jit(solution)/shard_map/ppermute | solution.py:503
  42.3 16.9 %collective-permute-done.2 = bf16[1,12,16,512]{3,2,1,0:T(8,128)(2,1)S(1)} collective-permute-done((bf16[1,12,16,512]{3,2,1,0:T(8,128)(2,1)S(1)}, bf16[1,12,16,512]{3,2,1,0:T(8,128)(2,1)S(1)}, u32[]{:S(2)}, u32[]{:S(2)}) %collective-permute-start.2) | collective-permute-done | bytes 196640 | tf_op jit(solution)/shard_map/ppermute | solution.py:503
  62.9 5.5 %collective-permute-done.3 = bf16[2,12,16,512]{3,2,1,0:T(8,128)(2,1)S(1)} collective-permute-done((bf16[2,12,16,512]{3,2,1,0:T(8,128)(2,1)S(1)}, bf16[2,12,16,512]{3,2,1,0:T(8,128)(2,1)S(1)}, u32[]{:S(2)}, u32[]{:S(2)}) %collective-permute-start.3) | collective-permute-done | bytes 393248 | tf_op jit(solution)/shard_map/ppermute | solution.py:503
  69.6 15.8 %collective-permute-done.4 = bf16[4,12,16,512]{3,2,1,0:T(8,128)(2,1)S(1)} collective-permute-done((bf16[4,12,16,512]{3,2,1,0:T(8,128)(2,1)S(1)}, bf16[4,12,16,512]{3,2,1,0:T(8,128)(2,1)S(1)}, u32[]{:S(2)}, u32[]{:S(2)}) %collective-permute-start.4) | collective-permute-done | bytes 786464 | tf_op jit(solution)/shard_map/ppermute | solution.py:503
  97.5 8.6 %collective-permute-done.5 = bf16[8,12,16,512]{3,2,1,0:T(8,128)(2,1)S(1)} collective-permute-done((bf16[8,12,16,512]{3,2,1,0:T(8,128)(2,1)S(1)}, bf16[8,12,16,512]{3,2,1,0:T(8,128)(2,1)S(1)}, u32[]{:S(2)}, u32[]{:S(2)}) %collective-permute-start.5) | collective-permute-done | bytes 1572896 | tf_op jit(solution)/shard_map/ppermute | solution.py:503
  110.7 57.6 %all-gather = bf16[128,4,256]{2,1,0:T(4,128)(2,1)} all-gather(bf16[1,4,256]{2,1,0:T(4,128)(2,1)S(1)} %bitcast.148), channel_id=1, replica_groups=mesh['x'=4,'c'=2,'y'=4,'z'=4] {'x','c','y','z'}, dimensions={0}, use_global_device_ids=true | all-gather | bytes 264192 | tf_op jit(solution)/shard_map/all_gather | solution.py:608
  177.2 4.8 %constant_dynamic-update-slice_fusion.23.gb = bf16[32,16,16,512]{3,2,1,0:T(8,128)(2,1)} fusion(bf16[32,16,16,512]{3,2,1,0:T(8,128)(2,1)} %copy-done.9, bf16[16,16,16,512]{3,2,1,0:T(8,128)(2,1)} %collective-permute-done.11), kind=kLoop, calls=%fused_computation.89 | loop fusion | bytes 8388608 | tf_op jit(solution)/shard_map/concatenate | solution.py:567
  182.0 52.0 %shard_map.433 = (bf16[384,512]{1,0:T(8,128)(2,1)}, bf16[32,8,16,512]{3,2,1,0:T(8,128)(2,1)}, f32[384,512]{1,0:T(8,128)}, f32[8,512]{1,0:T(8,128)}, f32[1,2048]{...) custom-call(s32[32]{0:T(128)} %get-tuple-element.149.tab_a, ...), custom_call_target="tpu_custom_call" | custom-call | flops 12000000000 | bytes 16777216 | tf_op jit(solution)/shard_map/pallas_call | solution.py:459
  234.0 3.1 slice.276
  237.1 3.5 collective-permute-start.26
  240.6 23.9 %shard_map.434 = (bf16[32,8,16,512]{3,2,1,0:T(8,128)(2,1)}, f32[384,512]{1,0:T(8,128)}, f32[384,512]{1,0:T(8,128)}, f32[128,512]{1,0:T(8,128)}) custom-call(s32[32]{0:T(128)} %get-tuple-element.148.tab_b, s32[1,5]{1,0:T(1,128)} %t_len.3, s32[1,5]{1,0:T(1,128)} %langs.3, f32[128,512]{1,0:T(8,128)} %convert_bitcast_fusion.vecs, ...), custom_call_target="tpu_custom_call" | custom-call | flops 6000000000 | bytes 16777216 | tf_op jit(solution)/shard_map/pallas_call | solution.py:459
  264.5 3.3 slice.259
  267.8 25.6 %shard_map.435 = (bf16[32,13,16,512]{3,2,1,0:T(8,128)(2,1)}, f32[384,512]{1,0:T(8,128)}) custom-call(s32[32]{0:T(128)} %get-tuple-element.149.tab_a, f32[128,512]{1,0:T(8,128)} %convert_bitcast_fusion.vecs, f32[1,2048]{1,0:T(1,128)} %reshape.236.b_enc, bf16[384,512]{1,0:T(8,128)(2,1)} %bitcast.155, f32[384,512]{1,0:T(8,128)} %get-tuple-element.72.g_memory, ...), custom_call_target="tpu_custom_call" | custom-call | flops 8000000000 | bytes 16777216 | tf_op jit(solution)/shard_map/pallas_call | solution.py:459
  302.8 2.9 collective-permute-start.20
  305.7 9.9 %collective-permute-done.27 = bf16[8,8,16,512]{3,2,1,0:T(8,128)(2,1)S(1)} collective-permute-done((bf16[8,8,16,512]{3,2,1,0:T(8,128)(2,1)S(1)}, bf16[8,8,16,512]{3,2,1,0:T(8,128)(2,1)S(1)}, u32[]{:S(2)}, u32[]{:S(2)}) %collective-permute-start.27) | collective-permute-done | bytes 1048608 | tf_op jit(solution)/shard_map/ppermute | solution.py:503
  316.2 16.3 %collective-permute-done.20 = bf16[8,8,16,512]{3,2,1,0:T(8,128)(2,1)S(1)} collective-permute-done((bf16[8,8,16,512]{3,2,1,0:T(8,128)(2,1)S(1)}, bf16[8,8,16,512]{3,2,1,0:T(8,128)(2,1)S(1)}, u32[]{:S(2)}, u32[]{:S(2)}) %collective-permute-start.20) | collective-permute-done | bytes 1048608 | tf_op jit(solution)/shard_map/ppermute | solution.py:503
  339.2 3.0 collective-permute-done.21
  344.0 17.1 %collective-permute-done.29 = bf16[2,8,16,512]{3,2,1,0:T(8,128)(2,1)} collective-permute-done((bf16[2,8,16,512]{3,2,1,0:T(8,128)(2,1)}, bf16[2,8,16,512]{3,2,1,0:T(8,128)(2,1)}, u32[]{:S(2)}, u32[]{:S(2)}) %collective-permute-start.29) | collective-permute-done | bytes 262176 | tf_op jit(solution)/shard_map/ppermute | solution.py:503
  382.1 5.2 %collective-permute-done.14 = bf16[4,13,16,512]{3,2,1,0:T(8,128)(2,1)S(1)} collective-permute-done((bf16[4,13,16,512]{3,2,1,0:T(8,128)(2,1)S(1)}, bf16[4,13,16,512]{3,2,1,0:T(8,128)(2,1)S(1)}, u32[]{:S(2)}, u32[]{:S(2)}) %collective-permute-start.14) | collective-permute-done | bytes 852000 | tf_op jit(solution)/shard_map/ppermute | solution.py:503
  390.0 10.6 %collective-permute-done.15 = bf16[2,13,16,512]{3,2,1,0:T(8,128)(2,1)S(1)} collective-permute-done((bf16[2,13,16,512]{3,2,1,0:T(8,128)(2,1)S(1)}, bf16[2,13,16,512]{3,2,1,0:T(8,128)(2,1)S(1)}, u32[]{:S(2)}, u32[]{:S(2)}) %collective-permute-start.15) | collective-permute-done | bytes 426016 | tf_op jit(solution)/shard_map/ppermute | solution.py:503
  400.9 5.8 %collective-permute-done.16 = bf16[1,13,16,512]{3,2,1,0:T(8,128)(2,1)S(1)} collective-permute-done((bf16[1,13,16,512]{3,2,1,0:T(8,128)(2,1)S(1)}, bf16[1,13,16,512]{3,2,1,0:T(8,128)(2,1)S(1)}, u32[]{:S(2)}, u32[]{:S(2)}) %collective-permute-start.16) | collective-permute-done | bytes 213024 | tf_op jit(solution)/shard_map/ppermute | solution.py:503
  410.2 3.7 collective-permute-done.17
  (218 shorter events, 101.5 us)
Async XLA Ops:
  10.6 10.7 %collective-permute-start.1 = (bf16[2,7,16,512]{3,2,0,1:T(8,128)(2,1)S(1)}, bf16[2,7,16,512]{3,2,0,1:T(8,128)(2,1)S(1)}, u32[]{:S(2)}, u32[]{:S(2)}) collective-permute-start(bf16[2,7,16,512]{3,2,0,1:T(8,128)(2,1)S(1)} %pad_maximum_fusion.8), channel_id=1, source_target_pairs={{0,3},{1,2},{2,1},{3,0},{4,7},{5,6},{6,5},{7,4},{8,11},{9,10},{10,... | collective-permute-start | bytes 688136 | tf_op jit(solution)/shard_map/ppermute | solution.py:503
  29.7 9.3 %collective-permute-start.8 = (bf16[2,16,16,512]{3,2,1,0:T(8,128)(2,1)S(1)}, bf16[2,16,16,512]{3,2,1,0:T(8,128)(2,1)S(1)}, u32[]{:S(2)}, u32[]{:S(2)}) collective-permute-start(bf16[2,16,16,512]{3,2,1,0:T(8,128)(2,1)S(1)} %pad_maximum_fusion.4), channel_id=1, source_target_pairs={{0,12},{1,13},{2,14},{3,15},{4,8},{5,9},{6,10},{7,11},{8,4},{9,5},... | collective-permute-start | bytes 1572872 | tf_op jit(solution)/shard_map/ppermute | solution.py:503
  40.0 19.8 %collective-permute-start.9 = (bf16[4,16,16,512]{3,2,1,0:T(8,128)(2,1)}, bf16[4,16,16,512]{3,2,1,0:T(8,128)(2,1)S(1)}, u32[]{:S(2)}, u32[]{:S(2)}) collective-permute-start(bf16[4,16,16,512]{3,2,1,0:T(8,128)(2,1)} %pad_maximum_fusion.2), channel_id=1, source_target_pairs={{0,32},{1,33},{2,34},{3,35},{4,36},{5,37},{6,38},{7,39},{8,40},{9,... | collective-permute-start | bytes 3145736 | tf_op jit(solution)/shard_map/ppermute | solution.py:503
  41.1 18.2 %collective-permute-start.2 = (bf16[1,12,16,512]{3,2,1,0:T(8,128)(2,1)S(1)}, bf16[1,12,16,512]{3,2,1,0:T(8,128)(2,1)S(1)}, u32[]{:S(2)}, u32[]{:S(2)}) collective-permute-start(bf16[1,12,16,512]{3,2,1,0:T(8,128)(2,1)S(1)} %maximum_bitcast_fusion.1), channel_id=1, source_target_pairs={{0,32},{1,33},{2,34},{3,35},{4,36},{5,37},{6,38},{7,39},{8,40},{9,... | collective-permute-start | bytes 589832 | tf_op jit(solution)/shard_map/ppermute | solution.py:503
  59.3 9.1 %collective-permute-start.3 = (bf16[2,12,16,512]{3,2,1,0:T(8,128)(2,1)S(1)}, bf16[2,12,16,512]{3,2,1,0:T(8,128)(2,1)S(1)}, u32[]{:S(2)}, u32[]{:S(2)}) collective-permute-start(bf16[2,12,16,512]{3,2,1,0:T(8,128)(2,1)S(1)} %pad_maximum_fusion.7), channel_id=1, source_target_pairs={{0,96},{1,97},{2,98},{3,99},{4,100},{5,101},{6,102},{7,103},{8,104... | collective-permute-start | bytes 1179656 | tf_op jit(solution)/shard_map/ppermute | solution.py:503
  60.1 30.8 %collective-permute-start.10 = (bf16[8,16,16,512]{3,2,1,0:T(8,128)(2,1)S(1)}, bf16[8,16,16,512]{3,2,1,0:T(8,128)(2,1)S(1)}, u32[]{:S(2)}, u32[]{:S(2)}) collective-permute-start(bf16[8,16,16,512]{3,2,1,0:T(8,128)(2,1)S(1)} %pad_maximum_fusion), channel_id=1, source_target_pairs={{0,96},{1,97},{2,98},{3,99},{4,100},{5,101},{6,102},{7,103},{8,104... | collective-permute-start | bytes 6291464 | tf_op jit(solution)/shard_map/ppermute | solution.py:503
  68.5 17.0 %collective-permute-start.4 = (bf16[4,12,16,512]{3,2,1,0:T(8,128)(2,1)S(1)}, bf16[4,12,16,512]{3,2,1,0:T(8,128)(2,1)S(1)}, u32[]{:S(2)}, u32[]{:S(2)}) collective-permute-start(bf16[4,12,16,512]{3,2,1,0:T(8,128)(2,1)S(1)} %pad_maximum_fusion.3), channel_id=1, source_target_pairs={{0,4},{1,5},{2,6},{3,7},{4,0},{5,1},{6,2},{7,3},{8,12},{9,13},{10,... | collective-permute-start | bytes 2359304 | tf_op jit(solution)/shard_map/ppermute | solution.py:503
  85.6 20.5 %collective-permute-start.5 = (bf16[8,12,16,512]{3,2,1,0:T(8,128)(2,1)S(1)}, bf16[8,12,16,512]{3,2,1,0:T(8,128)(2,1)S(1)}, u32[]{:S(2)}, u32[]{:S(2)}) collective-permute-start(bf16[8,12,16,512]{3,2,1,0:T(8,128)(2,1)S(1)} %pad_maximum_fusion.1), channel_id=1, source_target_pairs={{0,12},{1,13},{2,14},{3,15},{4,8},{5,9},{6,10},{7,11},{8,4},{9,5},... | collective-permute-start | bytes 4718600 | tf_op jit(solution)/shard_map/ppermute | solution.py:503
  92.8 84.3 %collective-permute-start.11 = (bf16[16,16,16,512]{3,2,1,0:T(8,128)(2,1)}, bf16[16,16,16,512]{3,2,1,0:T(8,128)(2,1)}, u32[]{:S(2)}, u32[]{:S(2)}) collective-permute-start(bf16[16,16,16,512]{3,2,1,0:T(8,128)(2,1)} %get-tuple-element.93), channel_id=1, source_target_pairs={{0,16},{1,17},{2,18},{3,19},{4,20},{5,21},{6,22},{7,23},{8,24},{9,... | collective-permute-start | bytes 12582920 | tf_op jit(solution)/shard_map/ppermute | solution.py:503
  110.4 64.6 %collective-permute-start.6 = (bf16[16,12,16,512]{3,2,1,0:T(8,128)(2,1)}, bf16[16,12,16,512]{3,2,1,0:T(8,128)(2,1)S(1)}, u32[]{:S(2)}, u32[]{:S(2)}) collective-permute-start(bf16[16,12,16,512]{3,2,1,0:T(8,128)(2,1)} %get-tuple-element.95), channel_id=1, source_target_pairs={{0,16},{1,17},{2,18},{3,19},{4,20},{5,21},{6,22},{7,23},{8,24},{9,... | collective-permute-start | bytes 9437192 | tf_op jit(solution)/shard_map/ppermute | solution.py:503
  237.1 59.4 %collective-permute-start.26 = (bf16[16,8,16,512]{3,2,1,0:T(8,128)(2,1)}, bf16[16,8,16,512]{3,2,1,0:T(8,128)(2,1)}, u32[]{:S(2)}, u32[]{:S(2)}) collective-permute-start(bf16[16,8,16,512]{3,2,1,0:T(8,128)(2,1)} %slice.276), channel_id=1, source_target_pairs={{0,16},{1,17},{2,18},{3,19},{4,20},{5,21},{6,22},{7,23},{8,24},{9,... | collective-permute-start | bytes 6291464 | tf_op jit(solution)/shard_map/ppermute | solution.py:503
  267.8 32.3 %collective-permute-start.19 = (bf16[16,8,16,512]{3,2,1,0:T(8,128)(2,1)}, bf16[16,8,16,512]{3,2,1,0:T(8,128)(2,1)}, u32[]{:S(2)}, u32[]{:S(2)}) collective-permute-start(bf16[16,8,16,512]{3,2,1,0:T(8,128)(2,1)} %slice.259), channel_id=1, source_target_pairs={{0,16},{1,17},{2,18},{3,19},{4,20},{5,21},{6,22},{7,23},{8,24},{9,... | collective-permute-start | bytes 6291464 | tf_op jit(solution)/shard_map/ppermute | solution.py:503
  295.9 37.1 %collective-permute-start.12 = (bf16[16,13,16,512]{3,2,1,0:T(8,128)(2,1)S(1)}, bf16[16,13,16,512]{3,2,1,0:T(8,128)(2,1)S(1)}, u32[]{:S(2)}, u32[]{:S(2)}) collective-permute-start(bf16[16,13,16,512]{3,2,1,0:T(8,128)(2,1)S(1)} %slice.234), channel_id=1, source_target_pairs={{0,16},{1,17},{2,18},{3,19},{4,20},{5,21},{6,22},{7,23},{8,24},{9,... | collective-permute-start | bytes 10223624 | tf_op jit(solution)/shard_map/ppermute | solution.py:503
  299.5 16.1 %collective-permute-start.27 = (bf16[8,8,16,512]{3,2,1,0:T(8,128)(2,1)S(1)}, bf16[8,8,16,512]{3,2,1,0:T(8,128)(2,1)S(1)}, u32[]{:S(2)}, u32[]{:S(2)}) collective-permute-start(bf16[8,8,16,512]{3,2,1,0:T(8,128)(2,1)S(1)} %slice.350), channel_id=1, source_target_pairs={{0,96},{1,97},{2,98},{3,99},{4,100},{5,101},{6,102},{7,103},{8,104... | collective-permute-start | bytes 3145736 | tf_op jit(solution)/shard_map/ppermute | solution.py:503
  302.8 29.7 %collective-permute-start.20 = (bf16[8,8,16,512]{3,2,1,0:T(8,128)(2,1)S(1)}, bf16[8,8,16,512]{3,2,1,0:T(8,128)(2,1)S(1)}, u32[]{:S(2)}, u32[]{:S(2)}) collective-permute-start(bf16[8,8,16,512]{3,2,1,0:T(8,128)(2,1)S(1)} %slice.338), channel_id=1, source_target_pairs={{0,96},{1,97},{2,98},{3,99},{4,100},{5,101},{6,102},{7,103},{8,104... | collective-permute-start | bytes 3145736 | tf_op jit(solution)/shard_map/ppermute | solution.py:503
  316.1 20.8 %collective-permute-start.28 = (bf16[4,8,16,512]{3,2,1,0:T(8,128)(2,1)S(1)}, bf16[4,8,16,512]{3,2,1,0:T(8,128)(2,1)S(1)}, u32[]{:S(2)}, u32[]{:S(2)}) collective-permute-start(bf16[4,8,16,512]{3,2,1,0:T(8,128)(2,1)S(1)} %slice.352), channel_id=1, source_target_pairs={{0,32},{1,33},{2,34},{3,35},{4,36},{5,37},{6,38},{7,39},{8,40},{9,... | collective-permute-start | bytes 1572872 | tf_op jit(solution)/shard_map/ppermute | solution.py:503
  332.9 9.3 %collective-permute-start.21 = (bf16[4,8,16,512]{3,2,1,0:T(8,128)(2,1)S(1)}, bf16[4,8,16,512]{3,2,1,0:T(8,128)(2,1)S(1)}, u32[]{:S(2)}, u32[]{:S(2)}) collective-permute-start(bf16[4,8,16,512]{3,2,1,0:T(8,128)(2,1)S(1)} %slice.340), channel_id=1, source_target_pairs={{0,32},{1,33},{2,34},{3,35},{4,36},{5,37},{6,38},{7,39},{8,40},{9,... | collective-permute-start | bytes 1572872 | tf_op jit(solution)/shard_map/ppermute | solution.py:503
  336.2 34.9 %collective-permute-start.13 = (bf16[8,13,16,512]{3,2,1,0:T(8,128)(2,1)}, bf16[8,13,16,512]{3,2,1,0:T(8,128)(2,1)}, u32[]{:S(2)}, u32[]{:S(2)}) collective-permute-start(bf16[8,13,16,512]{3,2,1,0:T(8,128)(2,1)} %slice.320), channel_id=1, source_target_pairs={{0,12},{1,13},{2,14},{3,15},{4,8},{5,9},{6,10},{7,11},{8,4},{9,5},... | collective-permute-start | bytes 5111816 | tf_op jit(solution)/shard_map/ppermute | solution.py:503
  337.9 23.3 %collective-permute-start.29 = (bf16[2,8,16,512]{3,2,1,0:T(8,128)(2,1)}, bf16[2,8,16,512]{3,2,1,0:T(8,128)(2,1)}, u32[]{:S(2)}, u32[]{:S(2)}) collective-permute-start(bf16[2,8,16,512]{3,2,1,0:T(8,128)(2,1)} %slice.354), channel_id=1, source_target_pairs={{0,12},{1,13},{2,14},{3,15},{4,8},{5,9},{6,10},{7,11},{8,4},{9,5},... | collective-permute-start | bytes 786440 | tf_op jit(solution)/shard_map/ppermute | solution.py:503
  343.3 22.0 %collective-permute-start.22 = (bf16[2,8,16,512]{3,2,1,0:T(8,128)(2,1)}, bf16[2,8,16,512]{3,2,1,0:T(8,128)(2,1)}, u32[]{:S(2)}, u32[]{:S(2)}) collective-permute-start(bf16[2,8,16,512]{3,2,1,0:T(8,128)(2,1)} %slice.342), channel_id=1, source_target_pairs={{0,12},{1,13},{2,14},{3,15},{4,8},{5,9},{6,10},{7,11},{8,4},{9,5},... | collective-permute-start | bytes 786440 | tf_op jit(solution)/shard_map/ppermute | solution.py:503
  374.6 12.8 %collective-permute-start.14 = (bf16[4,13,16,512]{3,2,1,0:T(8,128)(2,1)S(1)}, bf16[4,13,16,512]{3,2,1,0:T(8,128)(2,1)S(1)}, u32[]{:S(2)}, u32[]{:S(2)}) collective-permute-start(bf16[4,13,16,512]{3,2,1,0:T(8,128)(2,1)S(1)} %slice.322), channel_id=1, source_target_pairs={{0,4},{1,5},{2,6},{3,7},{4,0},{5,1},{6,2},{7,3},{8,12},{9,13},{10,... | collective-permute-start | bytes 2555912 | tf_op jit(solution)/shard_map/ppermute | solution.py:503
  378.3 10.7 %collective-permute-start.31 = (bf16[2,32,512]{2,1,0:T(8,128)(2,1)S(1)}, bf16[2,32,512]{2,1,0:T(8,128)(2,1)S(1)}, u32[]{:S(2)}, u32[]{:S(2)}) collective-permute-start(bf16[2,32,512]{2,1,0:T(8,128)(2,1)S(1)} %pad_maximum_fusion.12), channel_id=1, source_target_pairs={{0,3},{1,2},{2,1},{3,0},{4,7},{5,6},{6,5},{7,4},{8,11},{9,10},{10,... | collective-permute-start | bytes 196616 | tf_op jit(solution)/shard_map/ppermute | solution.py:503
  388.9 11.7 %collective-permute-start.15 = (bf16[2,13,16,512]{3,2,1,0:T(8,128)(2,1)S(1)}, bf16[2,13,16,512]{3,2,1,0:T(8,128)(2,1)S(1)}, u32[]{:S(2)}, u32[]{:S(2)}) collective-permute-start(bf16[2,13,16,512]{3,2,1,0:T(8,128)(2,1)S(1)} %slice.324), channel_id=1, source_target_pairs={{0,96},{1,97},{2,98},{3,99},{4,100},{5,101},{6,102},{7,103},{8,104... | collective-permute-start | bytes 1277960 | tf_op jit(solution)/shard_map/ppermute | solution.py:503
  389.0 11.8 %collective-permute-start.32 = (bf16[1,32,512]{2,1,0:T(8,128)(2,1)S(1)}, bf16[1,32,512]{2,1,0:T(8,128)(2,1)S(1)}, u32[]{:S(2)}, u32[]{:S(2)}) collective-permute-start(bf16[1,32,512]{2,1,0:T(8,128)(2,1)S(1)} %slice.360), channel_id=1, source_target_pairs={{0,1},{1,0},{2,3},{3,2},{4,5},{5,4},{6,7},{7,6},{8,9},{9,8},{10,11... | collective-permute-start | bytes 98312 | tf_op jit(solution)/shard_map/ppermute | solution.py:503
  (27 other events, 239.9 us)
